TPU v7x, 32 devices: a whole 2x2x4 slice. The times are simulated.
32 devices in a mesh: seq: 16 (over z, y, x), fsdp: 1, dp: 2 (over core).
Axes of the slice: x: 2, y: 2, z: 4, core: 2. Of those that a mesh axis runs over, the one named last changes fastest.
Arguments:
- query_rows: bfloat16 [1, 2048, 2048], P('fsdp', 'seq', 'dp'), may hold values from -32 to 32
- key_rows: bfloat16 [1, 2048, 2048], P('fsdp', 'seq', 'dp'), may hold values from -32 to 32
- value_rows: bfloat16 [1, 2048, 2048], P('fsdp', 'seq', 'dp'), may hold values from -6 to 6
- summary_keys: bfloat16 [1, 128, 2048], P('fsdp', 'seq', 'dp'), may hold values from -6 to 6
- summary_values: bfloat16 [1, 128, 2048], P('fsdp', 'seq', 'dp'), may hold values from -6 to 6
- out_grad: bfloat16 [1, 2048, 2048], P('fsdp', 'seq', 'dp'), may hold values from -6 to 6
- rel_bias: float32 [4, 16], P(None, 'fsdp'), may hold values from -2 to 2
- pattern: int32 [1, 16, 3], P('fsdp'), may hold values from -1 to 15, as said below
- block_view: int32 [1, 16], P('fsdp'), may hold values from 0 to 95, as said below
- summary_view: int32 [1, 128], P('fsdp'), may hold values from 0 to 95
Outputs:
- attended: bfloat16 [1, 2048, 2048], P('fsdp', 'seq', 'dp')
- query_grad: bfloat16 [1, 2048, 2048], P('fsdp', 'seq', 'dp')
- key_grad: bfloat16 [1, 2048, 2048], P('fsdp', 'seq', 'dp')
- value_grad: bfloat16 [1, 2048, 2048], P('fsdp', 'seq', 'dp')
- summary_key_grad: bfloat16 [1, 128, 2048], P('fsdp', 'seq', 'dp')
- summary_value_grad: bfloat16 [1, 128, 2048], P('fsdp', 'seq', 'dp')
- bias_grad: float32 [4, 16], P(None, 'fsdp')
Inputs may be any that keep to these rules, and one draw needn't show every extreme that they name: `pattern`: slot j of block b's list holds b + j - 1 or -1 (no block); slot 1 always holds b. `block_view`: blocks that follow each other have equal views or views one apart on the cycle of 96 views.
All inputs are finite; a program needn't handle non-finite values.
Results may differ from a plain program's by a relative error of at most 0.0074.
Values may be sent and summed in bfloat16 or wider, within the bound.
A program may use at most 64 MiB of HBM per device.

v0:
```python
import math

import jax
import jax.numpy as jnp
from jax import lax
from jax.sharding import PartitionSpec as P

HSIZE = 128
BLK = 128
NVIEW = 96
NREL = 4


NEG_FILL = -1e30
HIGH = lax.Precision.HIGHEST


def extended_2(cells, sides, width):
    for axis, dim in sides:
        count = lax.axis_size(axis)
        ends = count - 1
        head = lax.slice_in_dim(cells, 0, width, axis=dim)
        tail = lax.slice_in_dim(cells, cells.shape[dim] - width, cells.shape[dim], axis=dim)
        cells = jnp.concatenate(
            [
                lax.ppermute(tail, axis, [(i, (i + 1) % count) for i in range(ends)]),
                cells,
                lax.ppermute(head, axis, [((i + 1) % count, i) for i in range(ends)]),
            ],
            axis=dim,
        )
    return cells


def passed_along(shard, axis, by):
    peers = lax.axis_size(axis)
    pairs = [(i, i + by) for i in range(peers) if 0 <= i + by < peers]
    return lax.ppermute(shard, axis, pairs)


def cycle_class(view_a, view_b):
    distance = jnp.abs(view_a - view_b)
    distance = jnp.minimum(distance, NVIEW - distance)
    return (
        (distance >= 1).astype(jnp.int32)
        + (distance >= 2).astype(jnp.int32)
        + (distance >= 8).astype(jnp.int32)
    )


def pair_products(left_rows, win_side, sum_side):
    first_part = jnp.einsum(
        "nqhd,nkhd->nhqk", left_rows, win_side, preferred_element_type=jnp.float32
    )
    second_part = jnp.einsum(
        "nqhd,khd->nhqk", left_rows, sum_side, preferred_element_type=jnp.float32
    )
    return jnp.concatenate([first_part, second_part], axis=3)


def weighted_sum(weights, win_side, sum_side, split_at):
    first_part = jnp.einsum(
        "nhqk,nkhd->nqhd", weights[..., :split_at], win_side, preferred_element_type=jnp.float32
    )
    second_part = jnp.einsum(
        "nhqk,khd->nqhd", weights[..., split_at:], sum_side, preferred_element_type=jnp.float32
    )
    return first_part + second_part


def to_extended(window_grad, blocks_dev, local_heads):
    slots = window_grad.reshape(blocks_dev, 3, BLK, local_heads, HSIZE)
    widths = ((0, 2), (1, 1), (2, 0))
    return sum(
        (
            jnp.pad(slots[:, position], (widths[position], (0, 0), (0, 0), (0, 0)))
            for position in range(3)
        )
    )


def body(
    query_rows,
    key_rows,
    value_rows,
    summary_keys,
    summary_values,
    out_grad,
    rel_bias,
    pattern,
    block_view,
    summary_view,
):
    tok_rows = query_rows.shape[1]
    width = query_rows.shape[2]
    local_heads = width // HSIZE
    blocks_dev = tok_rows // BLK
    split_at = 3 * BLK
    score_scale = 1.0 / math.sqrt(HSIZE)
    seq_index = lax.axis_index("seq")
    head_start = lax.axis_index("dp") * local_heads
    first_block = seq_index * blocks_dev
    block_shape = (blocks_dev, BLK, local_heads, HSIZE)
    queries = query_rows[0].reshape(block_shape)
    grads_out = out_grad[0].reshape(block_shape)
    paired = jnp.stack([key_rows[0], value_rows[0]])
    extended = extended_2(paired, (("seq", 1),), BLK)
    ext_blocks = extended.reshape(2, blocks_dev + 2, BLK, local_heads, HSIZE)
    windows = jnp.concatenate([ext_blocks[:, :-2], ext_blocks[:, 1:-1], ext_blocks[:, 2:]], axis=2)
    keys_win = windows[0]
    values_win = windows[1]
    gathered = lax.all_gather(
        jnp.stack([summary_keys[0], summary_values[0]]), "seq", axis=1, tiled=True
    )
    gathered = gathered.reshape(2, -1, local_heads, HSIZE)
    keys_sum = gathered[0]
    values_sum = gathered[1]
    full_table = lax.all_gather(rel_bias, "fsdp", axis=1, tiled=True)
    bias_table = lax.dynamic_slice_in_dim(full_table, head_start, local_heads, 1)
    global_views = block_view[0]
    global_pattern = pattern[0]
    local_views = lax.dynamic_slice_in_dim(jnp.pad(global_views, 1), first_block, blocks_dev + 2)
    own_views = local_views[1:-1]
    near_views = jnp.stack([local_views[:-2], local_views[1:-1], local_views[2:]], axis=1)
    own_pattern = lax.dynamic_slice_in_dim(global_pattern, first_block, blocks_dev)
    class_ids = jnp.arange(NREL, dtype=jnp.int32)
    onehot_win = (cycle_class(own_views[:, None], near_views)[:, :, None] == class_ids).astype(
        jnp.float32
    )
    onehot_sum = (
        cycle_class(own_views[:, None], summary_view[0][None, :])[:, :, None] == class_ids
    ).astype(jnp.float32)
    bias_win = jnp.repeat(
        jnp.einsum("nsc,ch->nhs", onehot_win, bias_table, precision=HIGH), BLK, axis=2
    )
    bias_sum = jnp.einsum("nkc,ch->nhk", onehot_sum, bias_table, precision=HIGH)
    bias = jnp.concatenate([bias_win, bias_sum], axis=2)[:, :, None, :]
    summary_rows = keys_sum.shape[0]
    allowed = jnp.concatenate(
        [
            jnp.repeat(own_pattern >= 0, BLK, axis=1),
            jnp.ones((blocks_dev, summary_rows), dtype=bool),
        ],
        axis=1,
    )
    scores = pair_products(queries, keys_win, keys_sum) * score_scale + bias
    scores = jnp.where(allowed[:, None, None, :], scores, NEG_FILL)
    row_max = jnp.max(scores, axis=3, keepdims=True)
    lifted = jnp.exp(scores - row_max)
    row_total = jnp.sum(lifted, axis=3, keepdims=True)
    weights = lifted / row_total
    weights_low = weights.astype(jnp.bfloat16)
    attended = weighted_sum(weights_low, values_win, values_sum, split_at).astype(jnp.bfloat16)
    prob_grad = pair_products(grads_out, values_win, values_sum)
    row_delta = jnp.sum(weights * prob_grad, axis=3, keepdims=True)
    score_grad = weights * (prob_grad - row_delta)
    grad_low = score_grad.astype(jnp.bfloat16)
    query_grad = (weighted_sum(grad_low, keys_win, keys_sum, split_at) * score_scale).astype(
        jnp.bfloat16
    )
    win_key = jnp.einsum(
        "nhqk,nqhd->nkhd", grad_low[..., :split_at], queries, preferred_element_type=jnp.float32
    )
    win_value = jnp.einsum(
        "nhqk,nqhd->nkhd",
        weights_low[..., :split_at],
        grads_out,
        preferred_element_type=jnp.float32,
    )
    grads_ext = jnp.stack(
        [
            to_extended(win_key, blocks_dev, local_heads),
            to_extended(win_value, blocks_dev, local_heads),
        ]
    )
    own_grads = grads_ext[:, 1:-1]
    for offset in (1, -1):
        outgoing = grads_ext[:, -1] if offset == 1 else grads_ext[:, 0]
        incoming = passed_along(outgoing.reshape(2, BLK, width), "seq", offset)
        incoming = incoming.reshape(2, BLK, local_heads, HSIZE)
        if offset == 1:
            own_grads = own_grads.at[:, 0].add(incoming)
        else:
            own_grads = own_grads.at[:, -1].add(incoming)
    key_grad = (own_grads[0] * score_scale).astype(jnp.bfloat16)
    value_grad = own_grads[1].astype(jnp.bfloat16)
    summary_terms = jnp.stack(
        [
            jnp.einsum(
                "nhqk,nqhd->khd",
                grad_low[..., split_at:],
                queries,
                preferred_element_type=jnp.float32,
            ),
            jnp.einsum(
                "nhqk,nqhd->khd",
                weights_low[..., split_at:],
                grads_out,
                preferred_element_type=jnp.float32,
            ),
        ]
    )
    summary_owned = lax.psum_scatter(
        summary_terms.reshape(2, summary_rows, width), "seq", scatter_dimension=1, tiled=True
    )
    summary_key_grad = (summary_owned[0] * score_scale).astype(jnp.bfloat16)
    summary_value_grad = summary_owned[1].astype(jnp.bfloat16)
    column_sums = jnp.sum(score_grad, axis=2)
    slot_sums = jnp.sum(
        column_sums[..., :split_at].reshape(blocks_dev, local_heads, 3, BLK), axis=3
    )
    bias_mine = jnp.einsum("nhs,nsc->ch", slot_sums, onehot_win, precision=HIGH) + jnp.einsum(
        "nhk,nkc->ch", column_sums[..., split_at:], onehot_sum, precision=HIGH
    )
    bias_local = lax.dynamic_update_slice_in_dim(
        jnp.zeros(full_table.shape, jnp.float32), bias_mine, head_start, 1
    )
    bias_total = lax.psum(bias_local, ("seq", "fsdp", "dp"))
    per_device = full_table.shape[1] // lax.axis_size("fsdp")
    bias_grad = lax.dynamic_slice_in_dim(
        bias_total, lax.axis_index("fsdp") * per_device, per_device, 1
    )
    return (
        attended.reshape(1, tok_rows, width),
        query_grad.reshape(1, tok_rows, width),
        key_grad.reshape(1, tok_rows, width),
        value_grad.reshape(1, tok_rows, width),
        summary_key_grad[None],
        summary_value_grad[None],
        bias_grad,
    )


def solution(mesh):
    placed = (
        P("fsdp", "seq", "dp"),
        P("fsdp", "seq", "dp"),
        P("fsdp", "seq", "dp"),
        P("fsdp", "seq", "dp"),
        P("fsdp", "seq", "dp"),
        P("fsdp", "seq", "dp"),
        P(None, "fsdp"),
        P("fsdp", None, None),
        P("fsdp", None),
        P("fsdp", None),
    )
    return jax.shard_map(
        body,
        mesh=mesh,
        in_specs=placed,
        out_specs=(
            P("fsdp", "seq", "dp"),
            P("fsdp", "seq", "dp"),
            P("fsdp", "seq", "dp"),
            P("fsdp", "seq", "dp"),
            P("fsdp", "seq", "dp"),
            P("fsdp", "seq", "dp"),
            P(None, "fsdp"),
        ),
        check_vma=False,
    )
```

profile of v0, /device:TPU:0, one launch (start us, length us, event | category | flops | bytes accessed | tf_op | source)
XLA Modules:
  0.0 207.9 jit_solution(12363930419511612496)
XLA Ops:
  7.2 1.0 constant_dynamic-update-slice_fusion.1
  8.2 1.0 constant_dynamic-update-slice_fusion
  9.2 1.4 collective-permute-start.1
  10.6 6.3 %collective-permute-start = (bf16[2,128,1024]{2,1,0:T(8,128)(2,1)S(1)}, bf16[2,128,1024]{2,1,0:T(8,128)(2,1)}, u32[]{:S(2)}, u32[]{:S(2)}) collective-permute-start(bf16[2,128,1024]{2,1,0:T(8,128)(2,1)S(1)} %constant_dynamic-update-slice_fusion), channel_id=1, source_target_pairs={{0,2},{2,4},{4,6},{6,8},{8,10},{10,12},{12,14},{14,16},{16,18},{18... | collective-permute-start | bytes 1572872 | tf_op jit(solution)/shard_map/ppermute | solution.py:26
  16.9 0.9 compare_reduce_fusion
  17.9 0.7 pad_dynamic-slice_fusion
  18.6 0.6 slice.157
  19.2 1.4 fusion.33
  20.6 0.2 fusion.24
  20.9 0.8 pad_maximum_fusion.4
  21.7 52.6 %all_gather.4 = bf16[2,128,1024]{2,0,1:T(2,128)(2,1)S(1)} all-gather(bf16[2,8,1024]{2,0,1:T(2,128)(2,1)S(1)} %copy.122), channel_id=1, replica_groups=mesh['seq'=16,'fsdp'=1,'dp'=2] {'seq'}, dimensions={1}, use_global_device_ids=true | all-gather | bytes 557056 | tf_op jit(solution)/shard_map/all_gather | solution.py:112
  74.3 0.7 fusion.44
  75.0 0.7 fusion.36
  75.7 0.2 copy.174
  75.9 0.2 copy.175
  76.1 0.4 copy.128
  76.5 0.4 copy.167
  77.0 0.2 convolution_bitcast_fusion.8
  77.3 0.3 convolution_bitcast_fusion.7
  77.6 0.3 convolution_bitcast_fusion.4
  77.9 1.2 pad_maximum_fusion.1
  79.1 0.4 copy.176
  79.8 0.1 copy_dynamic-update-slice_fusion.1
  79.9 0.1 copy_dynamic-update-slice_fusion
  80.1 0.3 convolution_bitcast_fusion.1
  80.4 0.8 copy-done.4
  81.2 0.3 convolution_bitcast_fusion
  81.6 0.8 fusion.39
  82.4 0.9 fusion.3
  83.3 1.3 multiply_reduce_fusion
  84.6 1.8 fusion.16
  86.4 1.4 fusion.19
  87.8 0.4 fusion.14
  88.2 1.1 fusion.18
  89.3 0.4 fusion.13
  89.6 2.0 copy.148
  91.7 1.2 fusion.41
  92.9 2.1 %copy.168 = f32[1,1,128,8,128]{2,4,3,1,0:T(8,128)} copy(f32[1,1,128,8,128]{4,2,1,3,0:T(8,128)} %get-tuple-element.64) | data formatting | bytes 1048576
  95.1 2.1 %copy.169 = f32[1,1,128,8,128]{2,4,3,1,0:T(8,128)} copy(f32[1,1,128,8,128]{4,2,1,3,0:T(8,128)} %get-tuple-element.65) | data formatting | bytes 1048576
  97.2 1.0 copy.170
  98.2 0.2 copy.149
  98.4 1.1 pad_maximum_fusion.3
  99.5 0.1 fusion.42
  99.6 1.0 copy.171
  100.6 1.0 copy.172
  101.6 1.0 copy.173
  102.6 2.0 add_bitcast_fusion
  104.7 1.5 fusion.9
  106.2 1.4 collective-permute-start.3
  107.6 5.6 %collective-permute-start.2 = (f32[2,128,1024]{1,2,0:T(8,128)}, f32[2,128,1024]{1,2,0:T(8,128)}, u32[]{:S(2)}, u32[]{:S(2)}) collective-permute-start(f32[2,128,1024]{1,2,0:T(8,128)} %bitcast.54), channel_id=1, source_target_pairs={{0,2},{2,4},{4,6},{6,8},{8,10},{10,12},{12,14},{14,16},{16,18},{18... | collective-permute-start | bytes 3145736 | tf_op jit(solution)/shard_map/ppermute | solution.py:38
  113.2 0.4 convolution_bitcast_fusion.3
  113.7 0.9 fusion.7
  114.6 1.8 copy.151
  116.4 1.8 convolution_bitcast_fusion.6
  118.3 1.9 fusion.8
  120.1 1.8 copy.150
  122.0 0.3 fusion.23
  122.3 0.1 convolution_add_fusion
  122.5 72.2 %psum.7 = f32[4,16]{1,0:T(4,128)} all-reduce(f32[4,16]{1,0:T(4,128)S(1)} %dynamic_update_slice.3), channel_id=1, replica_groups=mesh['seq'=16,'fsdp'=1,'dp'=2] {'seq','fsdp','dp'}, use_global_device_ids=true, to_apply=%region_6.7 | all-reduce | flops 64 | bytes 512 | tf_op jit(solution)/shard_map/psum | solution.py:218
  194.7 1.8 fusion.12
  196.6 0.9 copy.152
  197.5 0.9 copy.153
  198.3 1.4 slice.253
  199.7 1.4 fusion.20
  (51 shorter events, 0.8 us)
Async XLA Ops:
  7.2 13.4 %copy-start = (f32[4,16]{1,0:T(4,128)S(1)}, f32[4,16]{1,0:T(4,128)}, u32[]{:S(2)}) copy-start(f32[4,16]{1,0:T(4,128)} %param.20) | copy-start | bytes 772
  7.2 191.2 %reduce-scatter.2.cloned.1.call-start = ((), (), s32[]{:S(2)}) async-start(), calls=%async_computation.1 | async-start | bytes 1114112 | tf_op jit(solution)/shard_map/reduce_scatter | solution.py:203
  9.2 65.8 %copy-start.15 = (s32[1,128]{1,0:T(1,128)S(1)}, s32[1,128]{1,0:T(1,128)}, u32[]{:S(2)}) copy-start(s32[1,128]{1,0:T(1,128)} %param.23) | copy-start | bytes 1540
  9.2 66.5 %copy-start.13 = (bf16[1,128,1024]{2,1,0:T(8,128)(2,1)S(1)}, bf16[1,128,1024]{2,1,0:T(8,128)(2,1)}, u32[]{:S(2)}) copy-start(bf16[1,128,1024]{2,1,0:T(8,128)(2,1)} %param.14) | copy-start | bytes 786436
  9.2 68.7 %collective-permute-start.1 = (bf16[2,128,1024]{2,1,0:T(8,128)(2,1)S(1)}, bf16[2,128,1024]{2,1,0:T(8,128)(2,1)S(1)}, u32[]{:S(2)}, u32[]{:S(2)}) collective-permute-start(bf16[2,128,1024]{2,1,0:T(8,128)(2,1)S(1)} %constant_dynamic-update-slice_fusion), channel_id=1, source_target_pairs={{2,0},{4,2},{6,4},{8,6},{10,8},{12,10},{14,12},{16,14},{18,16},{20... | collective-permute-start | bytes 1572872 | tf_op jit(solution)/shard_map/ppermute | solution.py:28
  10.6 67.3 %collective-permute-start = (bf16[2,128,1024]{2,1,0:T(8,128)(2,1)S(1)}, bf16[2,128,1024]{2,1,0:T(8,128)(2,1)}, u32[]{:S(2)}, u32[]{:S(2)}) collective-permute-start(bf16[2,128,1024]{2,1,0:T(8,128)(2,1)S(1)} %constant_dynamic-update-slice_fusion), channel_id=1, source_target_pairs={{0,2},{2,4},{4,6},{6,8},{8,10},{10,12},{12,14},{14,16},{16,18},{18... | collective-permute-start | bytes 1572872 | tf_op jit(solution)/shard_map/ppermute | solution.py:26
  21.6 54.2 %copy-start.14 = (bf16[1,128,1024]{2,1,0:T(8,128)(2,1)S(1)}, bf16[1,128,1024]{2,1,0:T(8,128)(2,1)}, u32[]{:S(2)}) copy-start(bf16[1,128,1024]{2,1,0:T(8,128)(2,1)} %param.19) | copy-start | bytes 786436
  76.5 2.6 %copy-start.6 = (bf16[1,128,1024]{1,2,0:T(8,128)(2,1)}, bf16[1,128,1024]{1,2,0:T(8,128)(2,1)S(1)}, u32[]{:S(2)}) copy-start(bf16[1,128,1024]{1,2,0:T(8,128)(2,1)S(1)} %copy.128) | copy-start | bytes 786436
  77.0 2.1 %copy-start.8 = (bf16[1,128,1024]{1,2,0:T(8,128)(2,1)}, bf16[1,128,1024]{1,2,0:T(8,128)(2,1)S(1)}, u32[]{:S(2)}) copy-start(bf16[1,128,1024]{1,2,0:T(8,128)(2,1)S(1)} %copy.167) | copy-start | bytes 786436
  80.1 1.2 copy-start.4
  86.4 1.8 copy-start.2
  86.4 2.9 %copy-start.1 = (bf16[1,8,128,512]{2,3,1,0:T(8,128)(2,1)}, bf16[1,8,128,512]{2,3,1,0:T(8,128)(2,1)S(1)}, u32[]{:S(2)}) copy-start(bf16[1,8,128,512]{2,3,1,0:T(8,128)(2,1)S(1)} %get-tuple-element.63) | copy-start | bytes 3145732
  92.9 4.3 %copy-start.12 = (f32[1,1,128,8,128]{4,2,1,3,0:T(8,128)S(1)}, f32[1,1,128,8,128]{4,2,1,3,0:T(8,128)}, u32[]{:S(2)}) copy-start(f32[1,1,128,8,128]{4,2,1,3,0:T(8,128)} %get-tuple-element.66) | copy-start | bytes 1572868
  92.9 5.3 %copy-start.10 = (f32[8,128,128]{1,2,0:T(8,128)S(1)}, f32[8,128,128]{1,2,0:T(8,128)}, u32[]{:S(2)}) copy-start(f32[8,128,128]{1,2,0:T(8,128)} %fusion.18) | copy-start | bytes 1572868
  95.1 3.3 %copy-start.11 = (f32[1,128,1024]{2,1,0:T(8,128)S(1)}, f32[1,128,1024]{2,1,0:T(8,128)}, u32[]{:S(2)}) copy-start(f32[1,128,1024]{2,1,0:T(8,128)} %copy.148) | copy-start | bytes 1572868
  104.6 8.6 %copy-start.3 = (bf16[1,8,128,512]{2,3,1,0:T(8,128)(2,1)S(1)}, bf16[1,8,128,512]{2,3,1,0:T(8,128)(2,1)}, u32[]{:S(2)}) copy-start(bf16[1,8,128,512]{2,3,1,0:T(8,128)(2,1)} %copy-done.2) | copy-start | bytes 3145732
  104.7 8.6 %copy-start.5 = (bf16[2,1,384,8,128]{4,2,3,1,0:T(8,128)(2,1)S(1)}, bf16[2,1,384,8,128]{4,2,3,1,0:T(8,128)(2,1)}, u32[]{:S(2)}) copy-start(bf16[2,1,384,8,128]{4,2,3,1,0:T(8,128)(2,1)} %copy-done.4) | copy-start | bytes 4718596
  106.2 7.5 %copy-start.9 = (bf16[1,128,1024]{1,2,0:T(8,128)(2,1)S(1)}, bf16[1,128,1024]{1,2,0:T(8,128)(2,1)}, u32[]{:S(2)}) copy-start(bf16[1,128,1024]{1,2,0:T(8,128)(2,1)} %copy-done.8) | copy-start | bytes 786436
  106.2 88.5 %collective-permute-start.3 = (f32[2,128,1024]{1,2,0:T(8,128)}, f32[2,128,1024]{1,2,0:T(8,128)}, u32[]{:S(2)}, u32[]{:S(2)}) collective-permute-start(f32[2,128,1024]{1,2,0:T(8,128)} %bitcast.56), channel_id=1, source_target_pairs={{2,0},{4,2},{6,4},{8,6},{10,8},{12,10},{14,12},{16,14},{18,16},{20... | collective-permute-start | bytes 3145736 | tf_op jit(solution)/shard_map/ppermute | solution.py:38
  107.6 87.1 %collective-permute-start.2 = (f32[2,128,1024]{1,2,0:T(8,128)}, f32[2,128,1024]{1,2,0:T(8,128)}, u32[]{:S(2)}, u32[]{:S(2)}) collective-permute-start(f32[2,128,1024]{1,2,0:T(8,128)} %bitcast.54), channel_id=1, source_target_pairs={{0,2},{2,4},{4,6},{6,8},{8,10},{10,12},{12,14},{14,16},{16,18},{18... | collective-permute-start | bytes 3145736 | tf_op jit(solution)/shard_map/ppermute | solution.py:38
  114.6 3.6 %copy-start.7 = (bf16[1,128,1024]{1,2,0:T(8,128)(2,1)S(1)}, bf16[1,128,1024]{1,2,0:T(8,128)(2,1)}, u32[]{:S(2)}) copy-start(bf16[1,128,1024]{1,2,0:T(8,128)(2,1)} %copy-done.6) | copy-start | bytes 786436
Sparse Core Ops, SparseCore 0:
  99.6 92.0 reduce-scatter.1
where the time goes:
time: 209 us; the launch traced here: 208 us
  blocking collectives  125 us (60%)
  local copies, waits for them, and re-layouts  25.9 us (12%)
  other arithmetic  17.6 us (8%)
  starting transfers between devices  14.8 us (7%)
  between operations  14.4 us (7%)
  matrix products  10.4 us (5%)
    psum x1, blocking collectives, body(): bias_total = lax.psum(bias_local, ('seq', 'fsdp', 'dp'))  72.2 us
    all_gather x1, blocking collectives, body(): lax.all_gather(jnp.stack([summary_keys[0], summary_values[0]]), 'seq', ax...  52.6 us
    unnamed x49, local copies, waits for them, and re-layouts  16.6 us
    ppermute x2, starting transfers between devices, passed_along(): return lax.ppermute(shard, axis, pairs)  7.04 us
    ppermute x1, starting transfers between devices, extended_2(): lax.ppermute(tail, axis, [(i, (i + 1) % count) for i in range(ends)])  6.27 us
  transfers between devices with their start and end apart: 5, of which 0 were waited for; matrix products, arithmetic and copies ran while one was open for 13% of the time, Pallas kernels for 0%

commit v1 on v0

v1 whole, which is shorter than its diff:
```python
import functools
import math

import jax
import jax.numpy as jnp
from jax import lax
from jax.experimental import pallas as pl
from jax.experimental.pallas import tpu as pltpu
from jax.sharding import PartitionSpec as P

HSIZE = 128
BLK = 128
NVIEW = 96
NREL = 4
NEG_FILL = -1e30
F32 = jnp.float32
BF16 = jnp.bfloat16


def cycle_class(view_a, view_b):
    distance = jnp.abs(view_a - view_b)
    distance = jnp.minimum(distance, NVIEW - distance)
    return (
        (distance >= 1).astype(jnp.int32)
        + (distance >= 2).astype(jnp.int32)
        + (distance >= 8).astype(jnp.int32)
    )


def dot_nt(a, b):
    return lax.dot_general(a, b, (((1,), (1,)), ((), ())), preferred_element_type=F32)


def dot_nn(a, b):
    return lax.dot_general(a, b, (((1,), (0,)), ((), ())), preferred_element_type=F32)


def dot_tn(a, b):
    return lax.dot_general(a, b, (((0,), (0,)), ((), ())), preferred_element_type=F32)


def kernel(
    sizes,
    q_ref, k_ref, v_ref, sk_ref, sv_ref, do_ref, tab_ref, pat_ref, bv_ref, view_ref,
    att_ref, dq_ref, dk_ref, dv_ref, dsk_ref, dsv_ref, db_ref,
    kx, vx, qg, dog, sum_out, sum_in, ksm, vsm, dkx, dvx, dks, dvs,
    stage, halo_out, halo_in, rs_out, rs_in, b_out, b_in, x_in,
    in_send, in_recv, kv_send, kv_recv, sum_send, sum_recv, out_send, out_recv,
    hg_send, hg_recv, rs_send, rs_recv, b_send, b_recv, x_send, x_recv,
):
    S, D, G, T, W, HG, SR = sizes
    planes = S // G
    WG = HG * HSIZE
    H = G * HG
    blocks_dev = T // BLK
    nblk = G * blocks_dev
    total_blocks = planes * nblk
    scale = 1.0 / math.sqrt(HSIZE)
    brows = b_out.shape[0]

    s = lax.axis_index("seq")
    dp = lax.axis_index("dp")
    plane = s // G
    lane = lax.rem(s, G)
    first = plane * G

    def remote(src, dst, send, recv, target):
        return pltpu.make_async_remote_copy(
            src_ref=src, dst_ref=dst, send_sem=send, recv_sem=recv,
            device_id=target, device_id_type=pl.DeviceIdType.MESH,
        )

    def landed(dst, sem):
        pltpu.make_async_copy(dst, dst, sem).wait()

    barrier = pltpu.get_barrier_semaphore()
    for d in range(1, S):
        pl.semaphore_signal(
            barrier, inc=1, device_id={"seq": lax.rem(s + d, S)},
            device_id_type=pl.DeviceIdType.MESH,
        )
    for d in range(1, D):
        pl.semaphore_signal(
            barrier, inc=1, device_id={"dp": lax.rem(dp + d, D)},
            device_id_type=pl.DeviceIdType.MESH,
        )
    sum_out[...] = jnp.concatenate(
        [sk_ref[0].astype(F32), sv_ref[0].astype(F32)], axis=0
    ).astype(BF16)
    pl.semaphore_wait(barrier, S - 1 + D - 1)

    def cols(index):
        return pl.ds(pl.multiple_of(index * WG, WG), WG)

    def rows_at(index, base):
        return pl.ds(pl.multiple_of(base + index * T, BLK), T)

    sends = []
    pairs = ((k_ref, kx, BLK), (v_ref, vx, BLK), (q_ref, qg, 0), (do_ref, dog, 0))

    def send_pairs(which):
        for a in which:
            src, dst, base = pairs[a]
            for d in range(1, G):
                to = lax.rem(lane + d, G)
                copy = remote(
                    src.at[0, :, cols(to)], dst.at[rows_at(lane, base), :],
                    in_send.at[a, d], in_recv.at[a, lane], {"seq": first + to},
                )
                copy.start()
                sends.append(copy)
            pltpu.make_async_copy(
                src.at[0, :, cols(lane)], dst.at[rows_at(lane, base), :], in_recv.at[a, lane]
            ).start()

    send_pairs((0, 1))
    for d in range(1, S):
        to = lax.rem(s + d, S)
        copy = remote(
            sum_out.at[:, cols(lax.rem(to, G))], sum_in.at[s],
            sum_send.at[d], sum_recv.at[s], {"seq": to},
        )
        copy.start()
        sends.append(copy)
    pltpu.make_async_copy(sum_out.at[:, cols(lane)], sum_in.at[s], sum_recv.at[s]).start()
    send_pairs((2, 3))

    dkx[...] = jnp.zeros_like(dkx)
    dvx[...] = jnp.zeros_like(dvx)
    dks[...] = jnp.zeros_like(dks)
    dvs[...] = jnp.zeros_like(dvs)

    has_prev = plane > 0
    has_next = plane < planes - 1
    top = (G * T, G * T + BLK)
    low = (BLK, 2 * BLK)
    last = (BLK + G * T, 2 * BLK + G * T)

    for a in range(2):
        for j in range(G):
            landed(pairs[a][1].at[pl.ds(BLK + j * T, T), :], in_recv.at[a, j])

    def halo_copy(a, forward):
        buf = (kx, vx)[a]
        if forward:
            return remote(
                buf.at[pl.ds(top[0], BLK), :], buf.at[pl.ds(0, BLK), :],
                kv_send.at[0, a], kv_recv.at[0, a], {"seq": lax.rem(s + G, S)},
            )
        return remote(
            buf.at[pl.ds(low[0], BLK), :], buf.at[pl.ds(last[0], BLK), :],
            kv_send.at[1, a], kv_recv.at[1, a], {"seq": lax.rem(s + S - G, S)},
        )

    @pl.when(has_next)
    def _():
        for a in range(2):
            halo_copy(a, True).start()

    @pl.when(has_prev)
    def _():
        for a in range(2):
            halo_copy(a, False).start()

    @pl.when(jnp.logical_not(has_prev))
    def _():
        for buf in (kx, vx):
            buf[0:BLK, :] = jnp.zeros((BLK, WG), BF16)

    @pl.when(jnp.logical_not(has_next))
    def _():
        for buf in (kx, vx):
            buf[last[0]:last[1], :] = jnp.zeros((BLK, WG), BF16)

    for j in range(S):
        landed(sum_in.at[j], sum_recv.at[j])
    both = sum_in[...].astype(F32)
    ksm[...] = both[:, :SR, :].reshape(S * SR, WG).astype(BF16)
    vsm[...] = both[:, SR:, :].reshape(S * SR, WG).astype(BF16)
    view_rows = jnp.broadcast_to(view_ref[...].astype(F32), (BLK, S * SR)).T.astype(jnp.int32)

    for a in (2, 3):
        for j in range(G):
            landed(pairs[a][1].at[pl.ds(j * T, T), :], in_recv.at[a, j])

    @pl.when(has_prev)
    def _():
        for a in range(2):
            landed((kx, vx)[a].at[pl.ds(0, BLK), :], kv_recv.at[0, a])

    @pl.when(has_next)
    def _():
        for a in range(2):
            landed((kx, vx)[a].at[pl.ds(last[0], BLK), :], kv_recv.at[1, a])

    bias_acc = [jnp.zeros((1, BLK), F32) for _ in range(HG * NREL)]

    def one_block(n):
        block = plane * nblk + n
        view = bv_ref[0, block]
        slot_class = []
        slot_open = []
        for j in range(3):
            near = jnp.clip(block + (j - 1), 0, total_blocks - 1)
            slot_class.append(cycle_class(view, bv_ref[0, near]))
            slot_open.append(pat_ref[0, block, j] >= 0)
        sum_class = cycle_class(view, view_rows)
        here = slice(n * BLK, (n + 1) * BLK)
        win = slice(n * BLK, (n + 3) * BLK)
        for h in range(HG):
            hc = slice(h * HSIZE, (h + 1) * HSIZE)
            head = dp * H + lane * HG + h
            table = [tab_ref[c, head] for c in range(NREL)]
            q = qg[here, hc]
            do = dog[here, hc]
            kw = kx[win, hc]
            vw = vx[win, hc]
            ks = ksm[:, hc]
            vs = vsm[:, hc]
            raw = dot_nt(kw, q)
            scores = []
            for j in range(3):
                c = slot_class[j]
                b = jnp.where(
                    c >= 2, jnp.where(c == 3, table[3], table[2]),
                    jnp.where(c == 1, table[1], table[0]),
                )
                b = jnp.where(slot_open[j], b, NEG_FILL)
                scores.append(raw[j * BLK:(j + 1) * BLK] * scale + b)
            sum_bias = jnp.where(
                sum_class >= 2, jnp.where(sum_class == 3, table[3], table[2]),
                jnp.where(sum_class == 1, table[1], table[0]),
            )
            scores.append(dot_nt(ks, q) * scale + sum_bias)
            top_score = functools.reduce(
                jnp.maximum, [jnp.max(x, axis=0, keepdims=True) for x in scores]
            )
            lifted = [jnp.exp(x - top_score) for x in scores]
            total = sum(jnp.sum(x, axis=0, keepdims=True) for x in lifted)
            inverse = 1.0 / total
            weights = [x * inverse for x in lifted]
            dpw = dot_nt(vw, do)
            prob = [dpw[j * BLK:(j + 1) * BLK] for j in range(3)] + [dot_nt(vs, do)]
            delta = sum(jnp.sum(w * x, axis=0, keepdims=True) for w, x in zip(weights, prob))
            grads = [w * (x - delta) for w, x in zip(weights, prob)]
            w_win = jnp.concatenate([w.astype(BF16) for w in weights[:3]], axis=0)
            w_sum = weights[3].astype(BF16)
            g_win = jnp.concatenate([g.astype(BF16) for g in grads[:3]], axis=0)
            g_sum = grads[3].astype(BF16)
            stage[0, here, hc] = (dot_tn(w_win, vw) + dot_tn(w_sum, vs)).astype(BF16)
            stage[1, here, hc] = ((dot_tn(g_win, kw) + dot_tn(g_sum, ks)) * scale).astype(BF16)
            dkx[win, hc] += dot_nn(g_win, q)
            dvx[win, hc] += dot_nn(w_win, do)
            dks[:, hc] += dot_nn(g_sum, q)
            dvs[:, hc] += dot_nn(w_sum, do)
            slot_sums = [jnp.sum(g, axis=0, keepdims=True) for g in grads[:3]]
            for c in range(NREL):
                term = jnp.sum(jnp.where(sum_class == c, grads[3], 0.0), axis=0, keepdims=True)
                for j in range(3):
                    term = term + slot_sums[j] * jnp.where(slot_class[j] == c, 1.0, 0.0)
                bias_acc[h * NREL + c] = bias_acc[h * NREL + c] + term

    outs = (att_ref, dq_ref, dk_ref, dv_ref)

    def out_copy(a, b):
        return remote(
            stage.at[a, pl.ds(b * T, T), :], outs[a].at[0, :, cols(lane)],
            out_send.at[a, b], out_recv.at[a, lane], {"seq": first + b},
        )

    def send_out(which, b):
        @pl.when(lane != b)
        def _():
            for a in which:
                out_copy(a, b).start()

        @pl.when(lane == b)
        def _():
            for a in which:
                pltpu.make_async_copy(
                    stage.at[a, pl.ds(b * T, T), :], outs[a].at[0, :, cols(lane)],
                    out_recv.at[a, lane],
                ).start()

    def halo_grad(back, a):
        i = (0 if back else 2) + a
        return remote(
            halo_out.at[i], halo_in.at[i], hg_send.at[i], hg_recv.at[i],
            {"seq": lax.rem(s + (S - G if back else G), S)},
        )

    def finish(b):
        span = slice(BLK + b * T, BLK + (b + 1) * T)
        stage[2, b * T:(b + 1) * T, :] = (dkx[span, :] * scale).astype(BF16)
        stage[3, b * T:(b + 1) * T, :] = dvx[span, :].astype(BF16)
        send_out((2, 3), b)

    order = list(dict.fromkeys([0, G - 1] + list(range(1, G - 1))))
    for b in order:
        for i in range(blocks_dev):
            one_block(b * blocks_dev + i)
        send_out((0, 1), b)
        if b == 0:
            halo_out[0] = dkx[0:BLK, :].astype(BF16)
            halo_out[1] = dvx[0:BLK, :].astype(BF16)

            @pl.when(has_prev)
            def _():
                for a in range(2):
                    halo_grad(True, a).start()
        if b == G - 1:
            halo_out[2] = dkx[last[0]:last[1], :].astype(BF16)
            halo_out[3] = dvx[last[0]:last[1], :].astype(BF16)

            @pl.when(has_next)
            def _():
                for a in range(2):
                    halo_grad(False, a).start()

    for b in range(1, G - 1):
        finish(b)

    packed = jnp.concatenate(
        [(dks[...] * scale).reshape(S, SR, WG), dvs[...].reshape(S, SR, WG)], axis=1
    )
    rs_out[...] = packed.astype(BF16)
    pad = brows - HG * NREL
    b_out[...] = jnp.concatenate(
        bias_acc + ([jnp.zeros((pad, BLK), F32)] if pad else []), axis=0
    )
    for d in range(1, S):
        to = lax.rem(s + d, S)
        copy = remote(b_out, b_in.at[s], b_send.at[d], b_recv.at[s], {"seq": to})
        copy.start()
        sends.append(copy)
        copy = remote(rs_out.at[to], rs_in.at[s], rs_send.at[d], rs_recv.at[s], {"seq": to})
        copy.start()
        sends.append(copy)
    pltpu.make_async_copy(b_out, b_in.at[s], b_recv.at[s]).start()
    pltpu.make_async_copy(rs_out.at[s], rs_in.at[s], rs_recv.at[s]).start()

    @pl.when(has_prev)
    def _():
        for a, buf in enumerate((dkx, dvx)):
            landed(halo_in.at[2 + a], hg_recv.at[2 + a])
            buf[low[0]:low[1], :] += halo_in[2 + a].astype(F32)

    @pl.when(has_next)
    def _():
        for a, buf in enumerate((dkx, dvx)):
            landed(halo_in.at[a], hg_recv.at[a])
            buf[top[0]:top[1], :] += halo_in[a].astype(F32)

    for b in sorted({0, G - 1}):
        finish(b)

    for j in range(S):
        landed(b_in.at[j], b_recv.at[j])
    x_in[dp] = jnp.sum(b_in[...].reshape(planes, G, brows, BLK), axis=0)
    for d in range(1, D):
        copy = remote(
            x_in.at[dp], x_in.at[dp], x_send.at[d], x_recv.at[dp], {"dp": lax.rem(dp + d, D)}
        )
        copy.start()
        sends.append(copy)

    for j in range(S):
        landed(rs_in.at[j], rs_recv.at[j])
    terms = jnp.sum(rs_in[...].astype(F32).reshape(planes, G, 2 * SR, WG), axis=0)
    for g in range(G):
        gc = slice(g * WG, (g + 1) * WG)
        dsk_ref[0, :, gc] = terms[g, :SR].astype(BF16)
        dsv_ref[0, :, gc] = terms[g, SR:].astype(BF16)

    for d in range(1, D):
        who = lax.rem(dp + d, D)
        landed(x_in.at[who], x_recv.at[who])
    lanes = lax.broadcasted_iota(jnp.int32, db_ref.shape, 1)
    result = jnp.zeros(db_ref.shape, F32)
    for e in range(D):
        for g in range(G):
            column = jnp.sum(x_in[e, g], axis=1, keepdims=True)
            for h in range(HG):
                at = e * H + g * HG + h
                result = jnp.where(lanes == at, column[h * NREL:(h + 1) * NREL], result)
    db_ref[...] = result

    for a in range(4):
        for j in range(G):
            landed(outs[a].at[0, :, pl.ds(j * WG, WG)], out_recv.at[a, j])

    for copy in sends:
        copy.wait_send()
    for b in range(G):
        @pl.when(lane != b)
        def _():
            for a in range(4):
                out_copy(a, b).wait_send()

    @pl.when(has_next)
    def _():
        for a in range(2):
            halo_copy(a, True).wait_send()
            halo_grad(False, a).wait_send()

    @pl.when(has_prev)
    def _():
        for a in range(2):
            halo_copy(a, False).wait_send()
            halo_grad(True, a).wait_send()


def body(
    query_rows, key_rows, value_rows, summary_keys, summary_values, out_grad,
    rel_bias, pattern, block_view, summary_view,
):
    S = lax.axis_size("seq")
    D = lax.axis_size("dp")
    F = lax.axis_size("fsdp")
    T, W = query_rows.shape[1:]
    SR = summary_keys.shape[1]
    heads = W // HSIZE
    G = next(g for g in (4, 2, 1) if S % g == 0 and heads % g == 0)
    HG = heads // G
    WG = HG * HSIZE
    brows = -(-HG * NREL // 8) * 8
    table = lax.all_gather(rel_bias, "fsdp", axis=1, tiled=True) if F > 1 else rel_bias
    rows_ext = G * T + 2 * BLK
    vmem = pl.BlockSpec(memory_space=pltpu.VMEM)
    smem = pl.BlockSpec(memory_space=pltpu.SMEM)
    dma = pltpu.SemaphoreType.DMA
    big = jax.ShapeDtypeStruct((1, T, W), BF16)
    small = jax.ShapeDtypeStruct((1, SR, W), BF16)
    results = pl.pallas_call(
        functools.partial(kernel, (S, D, G, T, W, HG, SR)),
        out_shape=(big, big, big, big, small, small, jax.ShapeDtypeStruct(table.shape, F32)),
        in_specs=[vmem] * 6 + [smem] * 3 + [vmem],
        out_specs=[vmem] * 7,
        scratch_shapes=[
            pltpu.VMEM((rows_ext, WG), BF16),
            pltpu.VMEM((rows_ext, WG), BF16),
            pltpu.VMEM((G * T, WG), BF16),
            pltpu.VMEM((G * T, WG), BF16),
            pltpu.VMEM((2 * SR, W), BF16),
            pltpu.VMEM((S, 2 * SR, WG), BF16),
            pltpu.VMEM((S * SR, WG), BF16),
            pltpu.VMEM((S * SR, WG), BF16),
            pltpu.VMEM((rows_ext, WG), F32),
            pltpu.VMEM((rows_ext, WG), F32),
            pltpu.VMEM((S * SR, WG), F32),
            pltpu.VMEM((S * SR, WG), F32),
            pltpu.VMEM((4, G * T, WG), BF16),
            pltpu.VMEM((4, BLK, WG), BF16),
            pltpu.VMEM((4, BLK, WG), BF16),
            pltpu.VMEM((S, 2 * SR, WG), BF16),
            pltpu.VMEM((S, 2 * SR, WG), BF16),
            pltpu.VMEM((brows, BLK), F32),
            pltpu.VMEM((S, brows, BLK), F32),
            pltpu.VMEM((D, G, brows, BLK), F32),
            dma((4, G)), dma((4, G)), dma((2, 2)), dma((2, 2)), dma((S,)), dma((S,)),
            dma((4, G)), dma((4, G)), dma((4,)), dma((4,)), dma((S,)), dma((S,)),
            dma((S,)), dma((S,)), dma((D,)), dma((D,)),
        ],
        compiler_params=pltpu.CompilerParams(
            collective_id=0, has_side_effects=True, vmem_limit_bytes=40 * 1024 * 1024
        ),
    )(
        query_rows, key_rows, value_rows, summary_keys, summary_values, out_grad,
        table, pattern, block_view, summary_view,
    )
    bias_grad = results[6]
    if F > 1:
        bias_total = lax.psum(bias_grad, "fsdp")
        part = table.shape[1] // F
        bias_grad = lax.dynamic_slice_in_dim(bias_total, lax.axis_index("fsdp") * part, part, 1)
    return (*results[:6], bias_grad)


def solution(mesh):
    rows = P("fsdp", "seq", "dp")
    placed = (
        rows, rows, rows, rows, rows, rows,
        P(None, "fsdp"), P("fsdp", None, None), P("fsdp", None), P("fsdp", None),
    )
    return jax.shard_map(
        body, mesh=mesh, in_specs=placed,
        out_specs=(rows, rows, rows, rows, rows, rows, P(None, "fsdp")),
        check_vma=False,
    )
```

time: 209 us -> 54.1 us (0.26)
  the two profiles are of different devices: /device:TPU:0 before, /device:TPU:5 now
where the time goes in v1:
time: 54.1 us; the launch traced here: 53.8 us
  Pallas kernels  42.5 us (79%)
  local copies, waits for them, and re-layouts  10.6 us (20%)
  between operations  0.69 us (1%)
    pallas_call x1, Pallas kernels, body(): pl.pallas_call(functools.partial(kernel, (S, D, G, T, W, HG, SR)), out_sh...  42.5 us
    unnamed x26, local copies, waits for them, and re-layouts  10.6 us

profile of v1, /device:TPU:5, one launch (start us, length us, event | category | flops | bytes accessed | tf_op | source)
XLA Modules:
  0.0 53.8 jit_solution(18076503221996324560)
XLA Ops:
  0.6 0.0 copy-start.8
  0.6 0.0 copy-start.7
  0.7 0.0 copy-start.6
  0.7 0.8 %copy.17.pat_ref = s32[1,16,3]{2,1,0:T(8,128)S(1)} copy(s32[1,16,3]{1,0,2:T(1,128)} %param.17) | data formatting | bytes 384 | tf_op args[7]
  1.4 0.0 copy-done.8
  1.4 0.0 copy-done.7
  1.4 0.0 copy-done.6
  1.4 0.0 copy-start
  1.5 0.9 %copy-done = bf16[1,128,1024]{2,1,0:T(8,128)(2,1)S(1)} copy-done((bf16[1,128,1024]{2,1,0:T(8,128)(2,1)S(1)}, bf16[1,128,1024]{2,1,0:T(8,128)(2,1)}, u32[]{:S(2)}) %copy-start) | copy-done | bytes 262168
  2.4 0.0 copy-start.1
  2.4 0.9 %copy-done.1 = bf16[1,128,1024]{2,1,0:T(8,128)(2,1)S(1)} copy-done((bf16[1,128,1024]{2,1,0:T(8,128)(2,1)S(1)}, bf16[1,128,1024]{2,1,0:T(8,128)(2,1)}, u32[]{:S(2)}) %copy-start.1) | copy-done | bytes 262168
  3.4 0.0 copy-start.2
  3.4 0.9 %copy-done.2 = bf16[1,128,1024]{2,1,0:T(8,128)(2,1)S(1)} copy-done((bf16[1,128,1024]{2,1,0:T(8,128)(2,1)S(1)}, bf16[1,128,1024]{2,1,0:T(8,128)(2,1)}, u32[]{:S(2)}) %copy-start.2) | copy-done | bytes 262168
  4.3 0.0 copy-start.3
  4.3 0.9 %copy-done.3 = bf16[1,128,1024]{2,1,0:T(8,128)(2,1)S(1)} copy-done((bf16[1,128,1024]{2,1,0:T(8,128)(2,1)S(1)}, bf16[1,128,1024]{2,1,0:T(8,128)(2,1)}, u32[]{:S(2)}) %copy-start.3) | copy-done | bytes 262168
  5.3 0.0 copy-start.4
  5.3 0.7 %copy-done.4 = bf16[1,8,1024]{2,1,0:T(8,128)(2,1)S(1)} copy-done((bf16[1,8,1024]{2,1,0:T(8,128)(2,1)S(1)}, bf16[1,8,1024]{2,1,0:T(8,128)(2,1)}, u32[]{:S(2)}) %copy-start.4) | copy-done | bytes 16408
  6.0 0.0 copy-start.5
  6.0 0.7 %copy-done.5 = bf16[1,8,1024]{2,1,0:T(8,128)(2,1)S(1)} copy-done((bf16[1,8,1024]{2,1,0:T(8,128)(2,1)S(1)}, bf16[1,8,1024]{2,1,0:T(8,128)(2,1)}, u32[]{:S(2)}) %copy-start.5) | copy-done | bytes 16408
  6.7 42.5 %shard_map.153 = (bf16[1,128,1024]{2,1,0:T(8,128)(2,1)S(1)}, bf16[1,128,1024]{2,1,0:T(8,128)(2,1)S(1)}, bf16[1,128,1024]{2,1,0:T(8,128)(2,1)S(1)}, bf16[1,128,10...) custom-call(bf16[1,128,1024]{2,1,0:T(8,128)(2,1)S(1)} %copy-done, ...), custom_call_target="tpu_custom_call" | custom-call | tf_op jit(solution)/shard_map/pallas_call | solution.py:434
  49.2 0.7 %copy.25 = bf16[1,128,1024]{2,1,0:T(8,128)(2,1)} copy(bf16[1,128,1024]{2,1,0:T(8,128)(2,1)S(1)} %get-tuple-element.14) | data formatting | bytes 524288
  49.9 0.7 %copy.26 = bf16[1,128,1024]{2,1,0:T(8,128)(2,1)} copy(bf16[1,128,1024]{2,1,0:T(8,128)(2,1)S(1)} %get-tuple-element.15) | data formatting | bytes 524288
  50.6 0.7 %copy.27 = bf16[1,128,1024]{2,1,0:T(8,128)(2,1)} copy(bf16[1,128,1024]{2,1,0:T(8,128)(2,1)S(1)} %get-tuple-element.16) | data formatting | bytes 524288
  51.3 0.7 %copy.28 = bf16[1,128,1024]{2,1,0:T(8,128)(2,1)} copy(bf16[1,128,1024]{2,1,0:T(8,128)(2,1)S(1)} %get-tuple-element.17) | data formatting | bytes 524288
  52.0 0.6 %copy.29 = bf16[1,8,1024]{2,1,0:T(8,128)(2,1)} copy(bf16[1,8,1024]{2,1,0:T(8,128)(2,1)S(1)} %get-tuple-element.18) | data formatting | bytes 32768
  52.6 0.6 %copy.30 = bf16[1,8,1024]{2,1,0:T(8,128)(2,1)} copy(bf16[1,8,1024]{2,1,0:T(8,128)(2,1)S(1)} %get-tuple-element.19) | data formatting | bytes 32768
  53.2 0.6 %copy.31 = f32[4,16]{1,0:T(4,128)} copy(f32[4,16]{1,0:T(4,128)S(1)} %get-tuple-element.20) | data formatting | bytes 512
Async XLA Ops:
  0.6 0.8 %copy-start.8 = (s32[1,128]{1,0:T(1,128)S(1)}, s32[1,128]{1,0:T(1,128)}, u32[]{:S(2)}) copy-start(s32[1,128]{1,0:T(1,128)} %view_ref.1) | copy-start | bytes 1540
  0.6 0.8 %copy-start.7 = (s32[1,16]{1,0:T(1,128)S(1)}, s32[1,16]{1,0:T(1,128)}, u32[]{:S(2)}) copy-start(s32[1,16]{1,0:T(1,128)} %bv_ref.1) | copy-start | bytes 196
  0.7 0.8 %copy-start.6 = (f32[4,16]{1,0:T(4,128)S(1)}, f32[4,16]{1,0:T(4,128)}, u32[]{:S(2)}) copy-start(f32[4,16]{1,0:T(4,128)} %tab_ref.1) | copy-start | bytes 772
  1.4 1.0 %copy-start = (bf16[1,128,1024]{2,1,0:T(8,128)(2,1)S(1)}, bf16[1,128,1024]{2,1,0:T(8,128)(2,1)}, u32[]{:S(2)}) copy-start(bf16[1,128,1024]{2,1,0:T(8,128)(2,1)} %q_ref.1) | copy-start | bytes 786436
  2.4 0.9 %copy-start.1 = (bf16[1,128,1024]{2,1,0:T(8,128)(2,1)S(1)}, bf16[1,128,1024]{2,1,0:T(8,128)(2,1)}, u32[]{:S(2)}) copy-start(bf16[1,128,1024]{2,1,0:T(8,128)(2,1)} %k_ref.1) | copy-start | bytes 786436
  3.4 0.9 %copy-start.2 = (bf16[1,128,1024]{2,1,0:T(8,128)(2,1)S(1)}, bf16[1,128,1024]{2,1,0:T(8,128)(2,1)}, u32[]{:S(2)}) copy-start(bf16[1,128,1024]{2,1,0:T(8,128)(2,1)} %v_ref.1) | copy-start | bytes 786436
  4.3 0.9 %copy-start.3 = (bf16[1,128,1024]{2,1,0:T(8,128)(2,1)S(1)}, bf16[1,128,1024]{2,1,0:T(8,128)(2,1)}, u32[]{:S(2)}) copy-start(bf16[1,128,1024]{2,1,0:T(8,128)(2,1)} %do_ref.1) | copy-start | bytes 786436
  5.3 0.7 %copy-start.4 = (bf16[1,8,1024]{2,1,0:T(8,128)(2,1)S(1)}, bf16[1,8,1024]{2,1,0:T(8,128)(2,1)}, u32[]{:S(2)}) copy-start(bf16[1,8,1024]{2,1,0:T(8,128)(2,1)} %sk_ref.1) | copy-start | bytes 49156
  6.0 0.7 %copy-start.5 = (bf16[1,8,1024]{2,1,0:T(8,128)(2,1)S(1)}, bf16[1,8,1024]{2,1,0:T(8,128)(2,1)}, u32[]{:S(2)}) copy-start(bf16[1,8,1024]{2,1,0:T(8,128)(2,1)} %sv_ref.1) | copy-start | bytes 49156

commit v2 on v1

--- a/solution.py
+++ b/solution.py
@@ -13,6 +13,7 @@
 NVIEW = 96
 NREL = 4
 NEG_FILL = -1e30
+LIMIT = 60 * 1024 * 1024
 F32 = jnp.float32
 BF16 = jnp.bfloat16
 
@@ -41,9 +42,9 @@
 
 def kernel(
     sizes,
-    q_ref, k_ref, v_ref, sk_ref, sv_ref, do_ref, tab_ref, pat_ref, bv_ref, view_ref,
-    att_ref, dq_ref, dk_ref, dv_ref, dsk_ref, dsv_ref, db_ref,
-    kx, vx, qg, dog, sum_out, sum_in, ksm, vsm, dkx, dvx, dks, dvs,
+    q_ref, k_ref, v_ref, sum_out, do_ref, tab_ref, pat_ref, bv_ref, view_ref,
+    att_ref, dq_ref, dk_ref, dv_ref, dsum_ref, db_ref,
+    kx, vx, qg, dog, sum_in, ksm, vsm, dkx, dvx, dks, dvs,
     stage, halo_out, halo_in, rs_out, rs_in, b_out, b_in, x_in,
     in_send, in_recv, kv_send, kv_recv, sum_send, sum_recv, out_send, out_recv,
     hg_send, hg_recv, rs_send, rs_recv, b_send, b_recv, x_send, x_recv,
@@ -84,46 +85,50 @@
             barrier, inc=1, device_id={"dp": lax.rem(dp + d, D)},
             device_id_type=pl.DeviceIdType.MESH,
         )
-    sum_out[...] = jnp.concatenate(
-        [sk_ref[0].astype(F32), sv_ref[0].astype(F32)], axis=0
-    ).astype(BF16)
     pl.semaphore_wait(barrier, S - 1 + D - 1)
 
     def cols(index):
         return pl.ds(pl.multiple_of(index * WG, WG), WG)
 
+    def head_cols(index, h):
+        return pl.ds(pl.multiple_of(index * WG + h * HSIZE, HSIZE), HSIZE)
+
     def rows_at(index, base):
         return pl.ds(pl.multiple_of(base + index * T, BLK), T)
 
     sends = []
     pairs = ((k_ref, kx, BLK), (v_ref, vx, BLK), (q_ref, qg, 0), (do_ref, dog, 0))
 
-    def send_pairs(which):
+    def send_pairs(which, h):
+        hc = pl.ds(h * HSIZE, HSIZE)
         for a in which:
             src, dst, base = pairs[a]
             for d in range(1, G):
                 to = lax.rem(lane + d, G)
                 copy = remote(
-                    src.at[0, :, cols(to)], dst.at[rows_at(lane, base), :],
-                    in_send.at[a, d], in_recv.at[a, lane], {"seq": first + to},
+                    src.at[0, :, head_cols(to, h)], dst.at[rows_at(lane, base), hc],
+                    in_send.at[a, h, d], in_recv.at[a, h, lane], {"seq": first + to},
                 )
                 copy.start()
                 sends.append(copy)
             pltpu.make_async_copy(
-                src.at[0, :, cols(lane)], dst.at[rows_at(lane, base), :], in_recv.at[a, lane]
+                src.at[0, :, head_cols(lane, h)], dst.at[rows_at(lane, base), hc],
+                in_recv.at[a, h, lane],
             ).start()
 
-    send_pairs((0, 1))
+    send_pairs((0, 1), 0)
     for d in range(1, S):
         to = lax.rem(s + d, S)
         copy = remote(
-            sum_out.at[:, cols(lax.rem(to, G))], sum_in.at[s],
+            sum_out.at[0, :, cols(lax.rem(to, G))], sum_in.at[s],
             sum_send.at[d], sum_recv.at[s], {"seq": to},
         )
         copy.start()
         sends.append(copy)
-    pltpu.make_async_copy(sum_out.at[:, cols(lane)], sum_in.at[s], sum_recv.at[s]).start()
-    send_pairs((2, 3))
+    pltpu.make_async_copy(sum_out.at[0, :, cols(lane)], sum_in.at[s], sum_recv.at[s]).start()
+    send_pairs((2, 3), 0)
+    for h in range(1, HG):
+        send_pairs((0, 1, 2, 3), h)
 
     dkx[...] = jnp.zeros_like(dkx)
     dvx[...] = jnp.zeros_like(dvx)
@@ -136,32 +141,6 @@
     low = (BLK, 2 * BLK)
     last = (BLK + G * T, 2 * BLK + G * T)
 
-    for a in range(2):
-        for j in range(G):
-            landed(pairs[a][1].at[pl.ds(BLK + j * T, T), :], in_recv.at[a, j])
-
-    def halo_copy(a, forward):
-        buf = (kx, vx)[a]
-        if forward:
-            return remote(
-                buf.at[pl.ds(top[0], BLK), :], buf.at[pl.ds(0, BLK), :],
-                kv_send.at[0, a], kv_recv.at[0, a], {"seq": lax.rem(s + G, S)},
-            )
-        return remote(
-            buf.at[pl.ds(low[0], BLK), :], buf.at[pl.ds(last[0], BLK), :],
-            kv_send.at[1, a], kv_recv.at[1, a], {"seq": lax.rem(s + S - G, S)},
-        )
-
-    @pl.when(has_next)
-    def _():
-        for a in range(2):
-            halo_copy(a, True).start()
-
-    @pl.when(has_prev)
-    def _():
-        for a in range(2):
-            halo_copy(a, False).start()
-
     @pl.when(jnp.logical_not(has_prev))
     def _():
         for buf in (kx, vx):
@@ -172,6 +151,54 @@
         for buf in (kx, vx):
             buf[last[0]:last[1], :] = jnp.zeros((BLK, WG), BF16)
 
+    def halo_copy(a, h, forward):
+        buf = (kx, vx)[a]
+        hc = pl.ds(h * HSIZE, HSIZE)
+        if forward:
+            return remote(
+                buf.at[pl.ds(top[0], BLK), hc], buf.at[pl.ds(0, BLK), hc],
+                kv_send.at[0, a, h], kv_recv.at[0, a, h], {"seq": lax.rem(s + G, S)},
+            )
+        return remote(
+            buf.at[pl.ds(low[0], BLK), hc], buf.at[pl.ds(last[0], BLK), hc],
+            kv_send.at[1, a, h], kv_recv.at[1, a, h], {"seq": lax.rem(s + S - G, S)},
+        )
+
+    def take_keys(h):
+        for a in range(2):
+            for j in range(G):
+                landed(
+                    pairs[a][1].at[pl.ds(BLK + j * T, T), pl.ds(h * HSIZE, HSIZE)],
+                    in_recv.at[a, h, j],
+                )
+
+        @pl.when(has_next)
+        def _():
+            for a in range(2):
+                halo_copy(a, h, True).start()
+
+        @pl.when(has_prev)
+        def _():
+            for a in range(2):
+                halo_copy(a, h, False).start()
+
+    def take_rest(h):
+        hc = pl.ds(h * HSIZE, HSIZE)
+        for a in (2, 3):
+            for j in range(G):
+                landed(pairs[a][1].at[pl.ds(j * T, T), hc], in_recv.at[a, h, j])
+
+        @pl.when(has_prev)
+        def _():
+            for a in range(2):
+                landed((kx, vx)[a].at[pl.ds(0, BLK), hc], kv_recv.at[0, a, h])
+
+        @pl.when(has_next)
+        def _():
+            for a in range(2):
+                landed((kx, vx)[a].at[pl.ds(last[0], BLK), hc], kv_recv.at[1, a, h])
+
+    take_keys(0)
     for j in range(S):
         landed(sum_in.at[j], sum_recv.at[j])
     both = sum_in[...].astype(F32)
@@ -179,23 +206,9 @@
     vsm[...] = both[:, SR:, :].reshape(S * SR, WG).astype(BF16)
     view_rows = jnp.broadcast_to(view_ref[...].astype(F32), (BLK, S * SR)).T.astype(jnp.int32)
 
-    for a in (2, 3):
-        for j in range(G):
-            landed(pairs[a][1].at[pl.ds(j * T, T), :], in_recv.at[a, j])
-
-    @pl.when(has_prev)
-    def _():
-        for a in range(2):
-            landed((kx, vx)[a].at[pl.ds(0, BLK), :], kv_recv.at[0, a])
-
-    @pl.when(has_next)
-    def _():
-        for a in range(2):
-            landed((kx, vx)[a].at[pl.ds(last[0], BLK), :], kv_recv.at[1, a])
-
     bias_acc = [jnp.zeros((1, BLK), F32) for _ in range(HG * NREL)]
 
-    def one_block(n):
+    def one_block(h, n):
         block = plane * nblk + n
         view = bv_ref[0, block]
         slot_class = []
@@ -207,7 +220,7 @@
         sum_class = cycle_class(view, view_rows)
         here = slice(n * BLK, (n + 1) * BLK)
         win = slice(n * BLK, (n + 3) * BLK)
-        for h in range(HG):
+        if True:
             hc = slice(h * HSIZE, (h + 1) * HSIZE)
             head = dp * H + lane * HG + h
             table = [tab_ref[c, head] for c in range(NREL)]
@@ -262,63 +275,94 @@
 
     outs = (att_ref, dq_ref, dk_ref, dv_ref)
 
-    def out_copy(a, b):
+    def out_parts(a, h, b):
+        return (
+            stage.at[a, pl.ds(b * T, T), pl.ds(h * HSIZE, HSIZE)],
+            outs[a].at[0, :, head_cols(lane, h)],
+        )
+
+    def out_copy(a, h, b):
+        src, dst = out_parts(a, h, b)
         return remote(
-            stage.at[a, pl.ds(b * T, T), :], outs[a].at[0, :, cols(lane)],
-            out_send.at[a, b], out_recv.at[a, lane], {"seq": first + b},
-        )
-
-    def send_out(which, b):
+            src, dst, out_send.at[a, h, b], out_recv.at[a, h, lane], {"seq": first + b}
+        )
+
+    def send_out(which, h, b):
         @pl.when(lane != b)
         def _():
             for a in which:
-                out_copy(a, b).start()
+                out_copy(a, h, b).start()
 
         @pl.when(lane == b)
         def _():
             for a in which:
-                pltpu.make_async_copy(
-                    stage.at[a, pl.ds(b * T, T), :], outs[a].at[0, :, cols(lane)],
-                    out_recv.at[a, lane],
-                ).start()
-
-    def halo_grad(back, a):
+                src, dst = out_parts(a, h, b)
+                pltpu.make_async_copy(src, dst, out_recv.at[a, h, lane]).start()
+
+    def halo_grad(back, a, h):
         i = (0 if back else 2) + a
         return remote(
-            halo_out.at[i], halo_in.at[i], hg_send.at[i], hg_recv.at[i],
+            halo_out.at[h, i], halo_in.at[h, i], hg_send.at[h, i], hg_recv.at[h, i],
             {"seq": lax.rem(s + (S - G if back else G), S)},
         )
 
-    def finish(b):
+    def finish(h, b):
         span = slice(BLK + b * T, BLK + (b + 1) * T)
-        stage[2, b * T:(b + 1) * T, :] = (dkx[span, :] * scale).astype(BF16)
-        stage[3, b * T:(b + 1) * T, :] = dvx[span, :].astype(BF16)
-        send_out((2, 3), b)
+        hc = slice(h * HSIZE, (h + 1) * HSIZE)
+        stage[2, b * T:(b + 1) * T, hc] = (dkx[span, hc] * scale).astype(BF16)
+        stage[3, b * T:(b + 1) * T, hc] = dvx[span, hc].astype(BF16)
+        send_out((2, 3), h, b)
+
+    def finish_ends(h):
+        hc = slice(h * HSIZE, (h + 1) * HSIZE)
+
+        @pl.when(has_prev)
+        def _():
+            for a, buf in enumerate((dkx, dvx)):
+                landed(halo_in.at[h, 2 + a], hg_recv.at[h, 2 + a])
+                buf[low[0]:low[1], hc] += halo_in[h, 2 + a].astype(F32)
+
+        @pl.when(has_next)
+        def _():
+            for a, buf in enumerate((dkx, dvx)):
+                landed(halo_in.at[h, a], hg_recv.at[h, a])
+                buf[top[0]:top[1], hc] += halo_in[h, a].astype(F32)
+
+        for b in sorted({0, G - 1}):
+            finish(h, b)
 
     order = list(dict.fromkeys([0, G - 1] + list(range(1, G - 1))))
-    for b in order:
-        for i in range(blocks_dev):
-            one_block(b * blocks_dev + i)
-        send_out((0, 1), b)
-        if b == 0:
-            halo_out[0] = dkx[0:BLK, :].astype(BF16)
-            halo_out[1] = dvx[0:BLK, :].astype(BF16)
-
-            @pl.when(has_prev)
-            def _():
-                for a in range(2):
-                    halo_grad(True, a).start()
-        if b == G - 1:
-            halo_out[2] = dkx[last[0]:last[1], :].astype(BF16)
-            halo_out[3] = dvx[last[0]:last[1], :].astype(BF16)
-
-            @pl.when(has_next)
-            def _():
-                for a in range(2):
-                    halo_grad(False, a).start()
-
-    for b in range(1, G - 1):
-        finish(b)
+    half = len(order) // 2
+    for h in range(HG):
+        hc = slice(h * HSIZE, (h + 1) * HSIZE)
+        take_rest(h)
+        for step, b in enumerate(order):
+            if step == half:
+                if h + 1 < HG:
+                    take_keys(h + 1)
+                if h > 0:
+                    finish_ends(h - 1)
+            for i in range(blocks_dev):
+                one_block(h, b * blocks_dev + i)
+            send_out((0, 1), h, b)
+            if b == 0:
+                halo_out[h, 0] = dkx[0:BLK, hc].astype(BF16)
+                halo_out[h, 1] = dvx[0:BLK, hc].astype(BF16)
+
+                @pl.when(has_prev)
+                def _():
+                    for a in range(2):
+                        halo_grad(True, a, h).start()
+            if b == G - 1:
+                halo_out[h, 2] = dkx[last[0]:last[1], hc].astype(BF16)
+                halo_out[h, 3] = dvx[last[0]:last[1], hc].astype(BF16)
+
+                @pl.when(has_next)
+                def _():
+                    for a in range(2):
+                        halo_grad(False, a, h).start()
+        for b in range(1, G - 1):
+            finish(h, b)
 
     packed = jnp.concatenate(
         [(dks[...] * scale).reshape(S, SR, WG), dvs[...].reshape(S, SR, WG)], axis=1
@@ -339,20 +383,7 @@
     pltpu.make_async_copy(b_out, b_in.at[s], b_recv.at[s]).start()
     pltpu.make_async_copy(rs_out.at[s], rs_in.at[s], rs_recv.at[s]).start()
 
-    @pl.when(has_prev)
-    def _():
-        for a, buf in enumerate((dkx, dvx)):
-            landed(halo_in.at[2 + a], hg_recv.at[2 + a])
-            buf[low[0]:low[1], :] += halo_in[2 + a].astype(F32)
-
-    @pl.when(has_next)
-    def _():
-        for a, buf in enumerate((dkx, dvx)):
-            landed(halo_in.at[a], hg_recv.at[a])
-            buf[top[0]:top[1], :] += halo_in[a].astype(F32)
-
-    for b in sorted({0, G - 1}):
-        finish(b)
+    finish_ends(HG - 1)
 
     for j in range(S):
         landed(b_in.at[j], b_recv.at[j])
@@ -369,8 +400,7 @@
     terms = jnp.sum(rs_in[...].astype(F32).reshape(planes, G, 2 * SR, WG), axis=0)
     for g in range(G):
         gc = slice(g * WG, (g + 1) * WG)
-        dsk_ref[0, :, gc] = terms[g, :SR].astype(BF16)
-        dsv_ref[0, :, gc] = terms[g, SR:].astype(BF16)
+        dsum_ref[0, :, gc] = terms[g].astype(BF16)
 
     for d in range(1, D):
         who = lax.rem(dp + d, D)
@@ -386,8 +416,11 @@
     db_ref[...] = result
 
     for a in range(4):
-        for j in range(G):
-            landed(outs[a].at[0, :, pl.ds(j * WG, WG)], out_recv.at[a, j])
+        for h in range(HG):
+            for j in range(G):
+                landed(
+                    outs[a].at[0, :, pl.ds(j * WG + h * HSIZE, HSIZE)], out_recv.at[a, h, j]
+                )
 
     for copy in sends:
         copy.wait_send()
@@ -395,19 +428,38 @@
         @pl.when(lane != b)
         def _():
             for a in range(4):
-                out_copy(a, b).wait_send()
+                for h in range(HG):
+                    out_copy(a, h, b).wait_send()
 
     @pl.when(has_next)
     def _():
         for a in range(2):
-            halo_copy(a, True).wait_send()
-            halo_grad(False, a).wait_send()
+            for h in range(HG):
+                halo_copy(a, h, True).wait_send()
+                halo_grad(False, a, h).wait_send()
 
     @pl.when(has_prev)
     def _():
         for a in range(2):
-            halo_copy(a, False).wait_send()
-            halo_grad(True, a).wait_send()
+            for h in range(HG):
+                halo_copy(a, h, False).wait_send()
+                halo_grad(True, a, h).wait_send()
+
+
+def store_kernel(a_in, b_in, c_in, d_in, sum_in, db_in, a, b, c, d, dsk, dsv, db, sems):
+    copies = [
+        pltpu.make_async_copy(src, dst, sems.at[i])
+        for i, (src, dst) in enumerate(((a_in, a), (b_in, b), (c_in, c), (d_in, d)))
+    ]
+    for copy in copies:
+        copy.start()
+    rows = dsk.shape[1]
+    both = sum_in[0].astype(F32)
+    dsk[0] = both[:rows].astype(BF16)
+    dsv[0] = both[rows:].astype(BF16)
+    db[...] = db_in[...]
+    for copy in copies:
+        copy.wait()
 
 
 def body(
@@ -429,19 +481,22 @@
     vmem = pl.BlockSpec(memory_space=pltpu.VMEM)
     smem = pl.BlockSpec(memory_space=pltpu.SMEM)
     dma = pltpu.SemaphoreType.DMA
+    anyspace = pl.BlockSpec(memory_space=pl.ANY)
+    bias = jax.ShapeDtypeStruct(table.shape, F32)
+    pair = jax.ShapeDtypeStruct((1, 2 * SR, W), BF16)
+    summaries = jnp.concatenate([summary_keys, summary_values], axis=1)
     big = jax.ShapeDtypeStruct((1, T, W), BF16)
     small = jax.ShapeDtypeStruct((1, SR, W), BF16)
     results = pl.pallas_call(
         functools.partial(kernel, (S, D, G, T, W, HG, SR)),
-        out_shape=(big, big, big, big, small, small, jax.ShapeDtypeStruct(table.shape, F32)),
-        in_specs=[vmem] * 6 + [smem] * 3 + [vmem],
-        out_specs=[vmem] * 7,
+        out_shape=(big, big, big, big, pair, bias),
+        in_specs=[anyspace] * 5 + [smem] * 3 + [vmem],
+        out_specs=[anyspace] * 4 + [vmem] * 2,
         scratch_shapes=[
             pltpu.VMEM((rows_ext, WG), BF16),
             pltpu.VMEM((rows_ext, WG), BF16),
             pltpu.VMEM((G * T, WG), BF16),
             pltpu.VMEM((G * T, WG), BF16),
-            pltpu.VMEM((2 * SR, W), BF16),
             pltpu.VMEM((S, 2 * SR, WG), BF16),
             pltpu.VMEM((S * SR, WG), BF16),
             pltpu.VMEM((S * SR, WG), BF16),
@@ -450,24 +505,34 @@
             pltpu.VMEM((S * SR, WG), F32),
             pltpu.VMEM((S * SR, WG), F32),
             pltpu.VMEM((4, G * T, WG), BF16),
-            pltpu.VMEM((4, BLK, WG), BF16),
-            pltpu.VMEM((4, BLK, WG), BF16),
+            pltpu.VMEM((HG, 4, BLK, HSIZE), BF16),
+            pltpu.VMEM((HG, 4, BLK, HSIZE), BF16),
             pltpu.VMEM((S, 2 * SR, WG), BF16),
             pltpu.VMEM((S, 2 * SR, WG), BF16),
             pltpu.VMEM((brows, BLK), F32),
             pltpu.VMEM((S, brows, BLK), F32),
             pltpu.VMEM((D, G, brows, BLK), F32),
-            dma((4, G)), dma((4, G)), dma((2, 2)), dma((2, 2)), dma((S,)), dma((S,)),
-            dma((4, G)), dma((4, G)), dma((4,)), dma((4,)), dma((S,)), dma((S,)),
+            dma((4, HG, G)), dma((4, HG, G)), dma((2, 2, HG)), dma((2, 2, HG)),
+            dma((S,)), dma((S,)), dma((4, HG, G)), dma((4, HG, G)),
+            dma((HG, 4)), dma((HG, 4)), dma((S,)), dma((S,)),
             dma((S,)), dma((S,)), dma((D,)), dma((D,)),
         ],
         compiler_params=pltpu.CompilerParams(
-            collective_id=0, has_side_effects=True, vmem_limit_bytes=40 * 1024 * 1024
+            collective_id=0, has_side_effects=True, vmem_limit_bytes=LIMIT
         ),
     )(
-        query_rows, key_rows, value_rows, summary_keys, summary_values, out_grad,
+        query_rows, key_rows, value_rows, summaries, out_grad,
         table, pattern, block_view, summary_view,
     )
+    whole = pl.BlockSpec((1, SR, W), lambda: (0, 0, 0))
+    table_block = pl.BlockSpec(table.shape, lambda: (0, 0))
+    results = pl.pallas_call(
+        store_kernel,
+        out_shape=(big, big, big, big, small, small, bias),
+        in_specs=[anyspace] * 4 + [vmem] * 2,
+        out_specs=[anyspace] * 4 + [whole, whole, table_block],
+        scratch_shapes=[dma((4,))],
+    )(*results)
     bias_grad = results[6]
     if F > 1:
         bias_total = lax.psum(bias_grad, "fsdp")

time: 54.1 us -> 76.6 us (1.42)
  the two profiles are of different devices: /device:TPU:5 before, /device:TPU:0 now
where the time goes in v2:
time: 76.6 us; the launch traced here: 76.2 us
  Pallas kernels  72.8 us (95%)
  local copies, waits for them, and re-layouts  1.35 us (2%)
  other arithmetic  1.35 us (2%)
    pallas_call x1, Pallas kernels, body(): pl.pallas_call(functools.partial(kernel, (S, D, G, T, W, HG, SR)), out_sh...  38.5 us
    pallas_call x1, Pallas kernels, body(): pl.pallas_call(store_kernel, out_shape=(big, big, big, big, small, small,...  34.3 us

profile of v2, /device:TPU:0, one launch (start us, length us, event | category | flops | bytes accessed | tf_op | source)
XLA Modules:
  0.0 76.2 jit_solution(2972267376021469398)
XLA Ops:
  0.6 1.4 %copy.17.pat_ref = s32[1,16,3]{2,1,0:T(8,128)} copy(s32[1,16,3]{1,0,2:T(1,128)} %param.17) | data formatting | bytes 384 | tf_op args[7]
  2.0 1.4 %pad_maximum_fusion.sum_out = bf16[1,16,1024]{2,1,0:T(8,128)(2,1)} fusion(bf16[1,8,1024]{2,1,0:T(8,128)(2,1)} %param.14, bf16[1,8,1024]{2,1,0:T(8,128)(2,1)} %param.13), kind=kLoop, calls=%fused_computation | loop fusion | flops 65536 | bytes 65536 | tf_op jit(solution)/shard_map/concatenate | solution.py:487
  3.3 38.5 %shard_map.153 = (bf16[1,128,1024]{2,1,0:T(8,128)(2,1)}, bf16[1,128,1024]{2,1,0:T(8,128)(2,1)}, bf16[1,128,1024]{2,1,0:T(8,128)(2,1)}, bf16[1,128,1024]{2,1,0:T(...) custom-call(bf16[1,128,1024]{2,1,0:T(8,128)(2,1)} %q_ref.1, bf16[1,128,1024]{2,1,0:T(8,128)(2,1)} %k_ref.1, ...), custom_call_target="tpu_custom_call" | custom-call | tf_op jit(solution)/shard_map/pallas_call | solution.py:490
  41.9 34.3 %shard_map.154 = (bf16[1,128,1024]{2,1,0:T(8,128)(2,1)}, bf16[1,128,1024]{2,1,0:T(8,128)(2,1)}, bf16[1,128,1024]{2,1,0:T(8,128)(2,1)}, bf16[1,128,1024]{2,1,0:T(...) custom-call(bf16[1,128,1024]{2,1,0:T(8,128)(2,1)} %get-tuple-element.13.a_in, ...), custom_call_target="tpu_custom_call" | custom-call | tf_op jit(solution)/shard_map/pallas_call | solution.py:529

commit v3 on v2

--- a/solution.py
+++ b/solution.py
@@ -446,18 +446,27 @@
                 halo_grad(True, a, h).wait_send()
 
 
-def store_kernel(a_in, b_in, c_in, d_in, sum_in, db_in, a, b, c, d, dsk, dsv, db, sems):
+def store_kernel(
+    a_in, b_in, c_in, d_in, sum_in, db_in, a, b, c, d, dsk, dsv, db, hold, in_sems, out_sems
+):
+    sources = (a_in, b_in, c_in, d_in)
+    loads = [
+        pltpu.make_async_copy(src, hold.at[i], in_sems.at[i]) for i, src in enumerate(sources)
+    ]
     copies = [
-        pltpu.make_async_copy(src, dst, sems.at[i])
-        for i, (src, dst) in enumerate(((a_in, a), (b_in, b), (c_in, c), (d_in, d)))
+        pltpu.make_async_copy(hold.at[i], dst, out_sems.at[i])
+        for i, dst in enumerate((a, b, c, d))
     ]
-    for copy in copies:
-        copy.start()
+    for load in loads:
+        load.start()
     rows = dsk.shape[1]
     both = sum_in[0].astype(F32)
     dsk[0] = both[:rows].astype(BF16)
     dsv[0] = both[rows:].astype(BF16)
     db[...] = db_in[...]
+    for load, copy in zip(loads, copies):
+        load.wait()
+        copy.start()
     for copy in copies:
         copy.wait()
 
@@ -531,7 +540,7 @@
         out_shape=(big, big, big, big, small, small, bias),
         in_specs=[anyspace] * 4 + [vmem] * 2,
         out_specs=[anyspace] * 4 + [whole, whole, table_block],
-        scratch_shapes=[dma((4,))],
+        scratch_shapes=[pltpu.VMEM((4, 1, T, W), BF16), dma((4,)), dma((4,))],
     )(*results)
     bias_grad = results[6]
     if F > 1:

time: 76.6 us -> 45.7 us (0.60)
  Pallas kernels: 72.8 us -> 41.9 us
    pallas_call x1, Pallas kernels: 34.3 us -> 3.35 us  [body(): pl.pallas_call(store_kernel, out_shape=(big, big, big, big, small, small,...]
where the time goes in v3:
time: 45.7 us; the launch traced here: 45.2 us
  Pallas kernels  41.9 us (92%)
  local copies, waits for them, and re-layouts  1.35 us (3%)
  other arithmetic  1.35 us (3%)
  between operations  0.64 us (1%)
    pallas_call x1, Pallas kernels, body(): pl.pallas_call(functools.partial(kernel, (S, D, G, T, W, HG, SR)), out_sh...  38.5 us
    pallas_call x1, Pallas kernels, body(): pl.pallas_call(store_kernel, out_shape=(big, big, big, big, small, small,...  3.35 us
    unnamed x1, local copies, waits for them, and re-layouts  1.35 us
    concatenate x1, other arithmetic, body(): summaries = jnp.concatenate([summary_keys, summary_values], axis=1)  1.35 us

profile of v3, /device:TPU:0, one launch (start us, length us, event | category | flops | bytes accessed | tf_op | source)
XLA Modules:
  0.0 45.2 jit_solution(1412610827529697024)
XLA Ops:
  0.6 1.4 %copy.17.pat_ref = s32[1,16,3]{2,1,0:T(8,128)} copy(s32[1,16,3]{1,0,2:T(1,128)} %param.17) | data formatting | bytes 384 | tf_op args[7]
  2.0 1.4 %pad_maximum_fusion.sum_out = bf16[1,16,1024]{2,1,0:T(8,128)(2,1)} fusion(bf16[1,8,1024]{2,1,0:T(8,128)(2,1)} %param.14, bf16[1,8,1024]{2,1,0:T(8,128)(2,1)} %param.13), kind=kLoop, calls=%fused_computation | loop fusion | flops 65536 | bytes 65536 | tf_op jit(solution)/shard_map/concatenate | solution.py:496
  3.3 38.5 %shard_map.153 = (bf16[1,128,1024]{2,1,0:T(8,128)(2,1)}, bf16[1,128,1024]{2,1,0:T(8,128)(2,1)}, bf16[1,128,1024]{2,1,0:T(8,128)(2,1)}, bf16[1,128,1024]{2,1,0:T(...) custom-call(bf16[1,128,1024]{2,1,0:T(8,128)(2,1)} %q_ref.1, bf16[1,128,1024]{2,1,0:T(8,128)(2,1)} %k_ref.1, ...), custom_call_target="tpu_custom_call" | custom-call | tf_op jit(solution)/shard_map/pallas_call | solution.py:499
  41.9 3.4 %shard_map.154 = (bf16[1,128,1024]{2,1,0:T(8,128)(2,1)}, bf16[1,128,1024]{2,1,0:T(8,128)(2,1)}, bf16[1,128,1024]{2,1,0:T(8,128)(2,1)}, bf16[1,128,1024]{2,1,0:T(...) custom-call(bf16[1,128,1024]{2,1,0:T(8,128)(2,1)} %get-tuple-element.13.a_in, ...), custom_call_target="tpu_custom_call" | custom-call | tf_op jit(solution)/shard_map/pallas_call | solution.py:538

commit v4 on v3

--- a/solution.py
+++ b/solution.py
@@ -372,6 +372,8 @@
     b_out[...] = jnp.concatenate(
         bias_acc + ([jnp.zeros((pad, BLK), F32)] if pad else []), axis=0
     )
+    finish_ends(HG - 1)
+
     for d in range(1, S):
         to = lax.rem(s + d, S)
         copy = remote(b_out, b_in.at[s], b_send.at[d], b_recv.at[s], {"seq": to})
@@ -382,8 +384,6 @@
         sends.append(copy)
     pltpu.make_async_copy(b_out, b_in.at[s], b_recv.at[s]).start()
     pltpu.make_async_copy(rs_out.at[s], rs_in.at[s], rs_recv.at[s]).start()
-
-    finish_ends(HG - 1)
 
     for j in range(S):
         landed(b_in.at[j], b_recv.at[j])

time: 45.7 us -> 46.3 us (1.013)
  Pallas kernels: 41.9 us -> 42.4 us
    pallas_call x1, Pallas kernels: 38.5 us -> 39 us  [body(): pl.pallas_call(functools.partial(kernel, (S, D, G, T, W, HG, SR)), out_sh...]
where the time goes in v4:
time: 46.3 us; the launch traced here: 45.7 us
  Pallas kernels  42.4 us (92%)
  local copies, waits for them, and re-layouts  1.35 us (3%)
  other arithmetic  1.35 us (3%)
  between operations  0.64 us (1%)
    pallas_call x1, Pallas kernels, body(): pl.pallas_call(functools.partial(kernel, (S, D, G, T, W, HG, SR)), out_sh...  39 us
    pallas_call x1, Pallas kernels, body(): pl.pallas_call(store_kernel, out_shape=(big, big, big, big, small, small,...  3.35 us
    unnamed x1, local copies, waits for them, and re-layouts  1.35 us
    concatenate x1, other arithmetic, body(): summaries = jnp.concatenate([summary_keys, summary_values], axis=1)  1.35 us

profile of v4, /device:TPU:0, one launch (start us, length us, event | category | flops | bytes accessed | tf_op | source)
XLA Modules:
  0.0 45.7 jit_solution(4517257238503666291)
XLA Ops:
  0.6 1.4 %copy.17.pat_ref = s32[1,16,3]{2,1,0:T(8,128)} copy(s32[1,16,3]{1,0,2:T(1,128)} %param.17) | data formatting | bytes 384 | tf_op args[7]
  2.0 1.4 %pad_maximum_fusion.sum_out = bf16[1,16,1024]{2,1,0:T(8,128)(2,1)} fusion(bf16[1,8,1024]{2,1,0:T(8,128)(2,1)} %param.14, bf16[1,8,1024]{2,1,0:T(8,128)(2,1)} %param.13), kind=kLoop, calls=%fused_computation | loop fusion | flops 65536 | bytes 65536 | tf_op jit(solution)/shard_map/concatenate | solution.py:496
  3.3 39.0 %shard_map.153 = (bf16[1,128,1024]{2,1,0:T(8,128)(2,1)}, bf16[1,128,1024]{2,1,0:T(8,128)(2,1)}, bf16[1,128,1024]{2,1,0:T(8,128)(2,1)}, bf16[1,128,1024]{2,1,0:T(...) custom-call(bf16[1,128,1024]{2,1,0:T(8,128)(2,1)} %q_ref.1, bf16[1,128,1024]{2,1,0:T(8,128)(2,1)} %k_ref.1, ...), custom_call_target="tpu_custom_call" | custom-call | tf_op jit(solution)/shard_map/pallas_call | solution.py:499
  42.4 3.4 %shard_map.154 = (bf16[1,128,1024]{2,1,0:T(8,128)(2,1)}, bf16[1,128,1024]{2,1,0:T(8,128)(2,1)}, bf16[1,128,1024]{2,1,0:T(8,128)(2,1)}, bf16[1,128,1024]{2,1,0:T(...) custom-call(bf16[1,128,1024]{2,1,0:T(8,128)(2,1)} %get-tuple-element.13.a_in, ...), custom_call_target="tpu_custom_call" | custom-call | tf_op jit(solution)/shard_map/pallas_call | solution.py:538
